TPU v7x, 32 devices: a whole 2x2x4 slice. The times are simulated.
32 devices in a mesh: win: 2 (over y), row: 4 (over z), col: 4 (over x, core).
Axes of the slice: x: 2, y: 2, z: 4, core: 2. Of those that a mesh axis runs over, the one named last changes fastest.
Arguments:
- records: bfloat16 [32, 4096, 1024], P('win', ('row', 'col'))
- tile_pairs: int32 [4, 4, 4, 2], P('row', 'col'), may hold values from 0 to 3
- tile_count: int32 [4, 4], P('row', 'col'), may hold values from 1 to 4, as said below
- bin_index: int32 [32], replicated, may hold values from 1 to 511, as said below
Outputs:
- cross_tiles: bfloat16 [4, 4, 4, 2, 32, 256, 256], P('row', 'col', 'win')
Inputs may be any that keep to these rules, and one draw needn't show every extreme that they name: Slots 0 to tile_count - 1 of a cell are live; some cell has all 4 live and some cell one. `bin_index`: distinct and increasing; the first is 1 and the last 511.
All inputs are finite; a program needn't handle non-finite values.
Results may differ from a plain program's by a relative error of at most 0.0069.
Values may be sent and summed in bfloat16 or wider, within the bound.
A program may use at most 256 MiB of HBM per device.

v0:
```python
import math
import jax
import jax.numpy as jnp
from jax import lax
from jax.sharding import PartitionSpec as P


def dft_table(bin_index, length):
    sample_ids = jnp.arange(length, dtype=jnp.int32)
    phases = sample_ids[:, None] * bin_index[None, :] % length
    angles = 2.0 * math.pi / length * phases.astype(jnp.float32)
    window_taper = 0.5 - 0.5 * jnp.cos(2.0 * math.pi / length * sample_ids.astype(jnp.float32))
    cosine = window_taper[:, None] * jnp.cos(angles)
    sine = -window_taper[:, None] * jnp.sin(angles)
    return jnp.concatenate([cosine, sine], axis=1).astype(jnp.bfloat16)


def cross_spectra(first_block, second_block):
    second_real = second_block[:, 0]
    second_imag = second_block[:, 1]
    stacked = jnp.stack(
        [
            jnp.stack([second_real, second_imag], axis=1),
            jnp.stack([-second_imag, second_real], axis=1),
        ],
        axis=0,
    )
    return jnp.einsum(
        "wcktp,ewcktq->tekpq", first_block, stacked, preferred_element_type=jnp.float32
    )


def body(records, tile_pairs, tile_count, bin_index):
    length = records.shape[2]
    chan_block = records.shape[1]
    kept_bins = bin_index.shape[0]
    phase_table = dft_table(bin_index, length)
    spectrum = jnp.einsum("wcs,sk->wkc", records, phase_table, preferred_element_type=jnp.float32)
    energy = jnp.sqrt(jnp.mean(spectrum * spectrum, axis=1, keepdims=True) + 1e-06)
    whitened = (spectrum / energy).astype(jnp.bfloat16)
    whitened = lax.all_gather(whitened, "win", axis=0, tiled=True)
    row_set = lax.all_gather(whitened, "col", axis=2, tiled=True)
    column_set = lax.all_gather(whitened, "row", axis=2, tiled=True)
    window_rows = whitened.shape[0]
    row_blocks = row_set.reshape(window_rows, 2, kept_bins, lax.axis_size("col"), chan_block)
    column_blocks = column_set.reshape(window_rows, 2, kept_bins, lax.axis_size("row"), chan_block)
    slot_pairs = tile_pairs[0, 0]
    live_count = tile_count[0, 0]
    owned_slots = slot_pairs.shape[0] // lax.axis_size("win")
    begin_row = lax.axis_index("win") * owned_slots
    chosen = lax.dynamic_slice_in_dim(slot_pairs, begin_row, owned_slots, 0)
    positions = begin_row + jnp.arange(owned_slots, dtype=jnp.int32)
    first_chosen = jnp.take(row_blocks, chosen[:, 0], axis=3)
    second_chosen = jnp.take(column_blocks, chosen[:, 1], axis=3)
    live_mask = (positions < live_count).astype(jnp.float32)
    summed = cross_spectra(first_chosen, second_chosen) * live_mask[:, None, None, None, None]
    return summed.astype(jnp.bfloat16).reshape(
        1, 1, owned_slots, 2, kept_bins, chan_block, chan_block
    )


def solution(mesh):
    return jax.shard_map(
        body,
        mesh=mesh,
        in_specs=(
            P("win", ("row", "col"), None),
            P("row", "col", None, None),
            P("row", "col"),
            P(),
        ),
        out_specs=P("row", "col", "win", None, None, None, None),
        check_vma=False,
    )
```

profile of v0, /device:TPU:0, one launch (start us, length us, event | category | flops | bytes accessed | tf_op | source)
XLA Modules:
  0.0 217.1 jit_solution(18415207110802437952)
XLA Ops:
  6.5 0.0 copy-start
  6.5 0.0 all-gather.4.cloned.1.call-start
  6.6 1.3 multiply_convert_fusion.1
  7.8 6.1 %multiply_reduce_fusion = (f32[16,256]{1,0:T(8,128)S(1)}, f32[64,16,256]{2,0,1:T(8,128)S(1)}) fusion(bf16[16,256,1024]{2,1,0:T(8,128)(2,1)} %param.6, bf16[1024,32]{0,1:T(8,128)(2,1)S(1)} %get-tuple-element.13, bf16[1024,32]{0,1:T(8,128)(2,1)S(1)} %get-tuple-element.12), kind=kOutput, calls=%fused_computation.14 | convolution fusion | flops 537653248 | bytes 9584640 | tf_op jit(solution)/shard_map/wcs,sk->wkc/dot_general | solution.py:38
  13.9 0.9 fusion.8
  14.8 0.0 all-gather.4.cloned.1.call-update
  14.9 0.0 all-gather.6.cloned.1.call-start
  14.9 24.1 %all-gather.4.cloned.1.call-done = bf16[32,64,256]{2,1,0:T(8,128)(2,1)} async-done(((bf16[16,64,256]{2,1,0:T(8,128)(2,1)}), bf16[32,64,256]{2,1,0:T(8,128)(2,1)}) %all-gather.4.cloned.1.call-update) | async-done | bytes 1048592 | tf_op jit(solution)/shard_map/all_gather | solution.py:41
  39.0 0.0 all-gather.6.cloned.1.call-update
  39.0 0.0 all-gather.8.cloned.1.call-start
  39.1 0.7 all-gather.8.cloned.1.call-update
  40.4 0.0 copy-done
  40.4 0.1 constant_dynamic-slice_fusion
  40.5 0.1 copy.20
  40.6 0.2 slice_reduce_fusion
  40.9 80.3 %all-gather.6.cloned.1.call-done = bf16[32,64,1024]{2,1,0:T(8,128)(2,1)} async-done(((bf16[32,64,256]{2,1,0:T(8,128)(2,1)}), bf16[32,64,1024]{2,1,0:T(8,128)(2,1)}) %all-gather.6.cloned.1.call-update) | async-done | bytes 4194320 | tf_op jit(solution)/shard_map/all_gather | solution.py:43
  121.2 7.9 %reshape.42 = bf16[32,2,32,4,256]{4,3,2,1,0:T(4,128)(2,1)} reshape(bf16[32,64,1024]{2,1,0:T(8,128)(2,1)} %all-gather.6.cloned.1.call-done) | data formatting | bytes 8388608 | tf_op jit(solution)/shard_map/reshape | solution.py:46
  129.1 5.3 %copy.21 = bf16[32,2,32,4,256]{4,2,1,0,3:T(8,128)(2,1)} copy(bf16[32,2,32,4,256]{4,3,2,1,0:T(4,128)(2,1)} %reshape.42) | data formatting | bytes 8388608 | tf_op jit(solution)/shard_map/reshape | solution.py:46
  134.4 21.6 %all-gather.8.cloned.1.call-done = bf16[32,64,1024]{2,1,0:T(8,128)(2,1)} async-done(((bf16[32,64,256]{2,1,0:T(8,128)(2,1)}), bf16[32,64,1024]{2,1,0:T(8,128)(2,1)}) %all-gather.8.cloned.1.call-update) | async-done | bytes 4194320 | tf_op jit(solution)/shard_map/all_gather | solution.py:42
  156.0 7.8 %reshape.43 = bf16[32,2,32,4,256]{4,3,2,1,0:T(4,128)(2,1)} reshape(bf16[32,64,1024]{2,1,0:T(8,128)(2,1)} %all-gather.8.cloned.1.call-done) | data formatting | bytes 8388608 | tf_op jit(solution)/shard_map/reshape | solution.py:45
  163.8 4.9 %copy.24 = bf16[32,2,32,4,256]{4,2,1,0,3:T(8,128)(2,1)} copy(bf16[32,2,32,4,256]{4,3,2,1,0:T(4,128)(2,1)} %reshape.43) | data formatting | bytes 8388608 | tf_op jit(solution)/shard_map/reshape | solution.py:45
  168.8 2.9 %gather_fusion = bf16[2,32,2,32,256]{4,3,2,1,0:T(8,128)(2,1)S(1)} fusion(bf16[32,2,32,4,256]{4,2,1,0,3:T(8,128)(2,1)} %copy.21, s32[1024]{0:T(1024)S(1)} %pad_clamp_fusion.1), kind=kCustom, calls=%fused_computation.clone | custom fusion | bytes 4194312 | tf_op jit(solution)/shard_map/jit(_take)/gather | solution.py:54
  171.6 2.7 %fusion.6 = (bf16[1,32,2,32,2,256]{5,1,2,0,3,4:T(8,128)(2,1)}, bf16[32,2,32,2,256]{4,0,1,2,3:T(8,128)(2,1)S(1)}) fusion(bf16[2,32,2,32,256]{4,3,2,1,0:T(8,128)(2,1)S(1)} %gather_fusion, pred[2]{0:T(512)(128)(4,1)S(1)} %get-tuple-element.19), kind=kLoop, calls=%fused_computation.15 | loop fusion | flops 1048576 | bytes 6291458 | tf_op jit(solution)/shard_map/stack | solution.py:21
  174.3 1.1 slice_negate_fusion
  175.4 2.9 %gather_fusion.1 = bf16[2,32,2,32,256]{4,3,2,1,0:T(8,128)(2,1)S(1)} fusion(bf16[32,2,32,4,256]{4,2,1,0,3:T(8,128)(2,1)} %copy.24, s32[1024]{0:T(1024)S(1)} %pad_clamp_fusion), kind=kCustom, calls=%fused_computation.1.clone | custom fusion | bytes 4194312 | tf_op jit(solution)/shard_map/jit(_take)/gather | solution.py:53
  178.3 0.0 copy-start.2
  178.3 0.3 select_bitcast_fusion
  178.5 0.9 copy-done.2
  179.5 0.0 copy-start.3
  179.5 0.2 maximum_bitcast_fusion
  179.7 1.3 copy-done.3
  181.1 8.2 %fusion.1 = bf16[1,1,2,2,32,256,256]{5,6,3,4,2,1,0:T(8,128)(2,1)} fusion(f32[2]{0:T(128)S(1)} %compare_convert_fusion, bf16[1,32,2,32,2,256]{5,1,2,0,3,4:T(8,128)(2,1)S(1)} %maximum_bitcast_fusion, bf16[1,32,2,32,2,256]{5,1,2,0,3,4:T(8,128)(2,1)S(1)} %copy-done.3, bf16[32,2,32,2,256,1]{4,2,1,0,3,5:T(8,128)(2,1)S(1)} %select_bitcast_fusion), kind=kOutput, calls=%fused_computation.4 | convolution fusion | flops 1092616192 | bytes 23068680 | tf_op jit(solution)/shard_map/wcktp,ewcktq->tekpq/dot_general | solution.py:28
  189.3 0.0 copy-start.1
  189.3 21.2 %copy.26 = bf16[1,1,2,2,32,256,256]{6,5,4,3,2,1,0:T(8,128)(2,1)} copy(bf16[1,1,2,2,32,256,256]{5,6,3,4,2,1,0:T(8,128)(2,1)} %fusion.1) | data formatting | bytes 33554432 | tf_op jit(solution)/shard_map/reshape | solution.py:57
  210.5 0.0 copy-done.1
  (8 shorter events, 0.1 us)
Async XLA Ops:
  6.5 33.9 %copy-start = (s32[1,1,4,2]{2,3,1,0:T(2,128)S(1)}, s32[1,1,4,2]{2,3,1,0:T(2,128)}, u32[]{:S(2)}) copy-start(s32[1,1,4,2]{2,3,1,0:T(2,128)} %param.7) | copy-start | bytes 100
  6.5 32.5 %all-gather.4.cloned.1.call-start = ((), (), s32[]{:S(2)}) async-start(), calls=%async_computation | async-start | bytes 1572864 | tf_op jit(solution)/shard_map/all_gather | solution.py:41
  14.9 106.3 %all-gather.6.cloned.1.call-start = ((), (), s32[]{:S(2)}) async-start(), calls=%async_computation.1 | async-start | bytes 5242880 | tf_op jit(solution)/shard_map/all_gather | solution.py:43
  39.0 116.9 %all-gather.8.cloned.1.call-start = ((), (), s32[]{:S(2)}) async-start(), calls=%async_computation.2 | async-start | bytes 5242880 | tf_op jit(solution)/shard_map/all_gather | solution.py:42
  178.3 1.2 copy-start.2
  179.5 1.6 copy-start.3
  189.3 21.2 %copy-start.1 = (s32[1,1,4,2]{2,3,1,0:T(2,128)S(1)}, s32[1,1,4,2]{2,3,1,0:T(2,128)}, u32[]{:S(2)}) copy-start(s32[1,1,4,2]{2,3,1,0:T(2,128)} %param.7) | copy-start | bytes 100
Sparse Core Ops, SparseCore 0:
  15.0 23.9 all-gather.3
  40.6 80.5 all-gather.5
  122.7 33.1 all-gather.7
where the time goes:
time: 218 us; the launch traced here: 217 us
  waiting for transfers between devices  127 us (58%)
  local copies, waits for them, and re-layouts  55.6 us (26%)
  matrix products  14.3 us (7%)
  between operations  13.9 us (6%)
  other arithmetic  6.51 us (3%)
    all_gather x1, waiting for transfers between devices, body(): column_set = lax.all_gather(whitened, 'row', axis=2, tiled=True)  80.3 us
    all_gather x1, waiting for transfers between devices, body(): whitened = lax.all_gather(whitened, 'win', axis=0, tiled=True)  24.1 us
    all_gather x1, waiting for transfers between devices, body(): row_set = lax.all_gather(whitened, 'col', axis=2, tiled=True)  21.6 us
    reshape x1, local copies, waits for them, and re-layouts, body(): summed.astype(jnp.bfloat16)  21.2 us
    reshape x2, local copies, waits for them, and re-layouts, body(): column_set.reshape(window_rows, 2, kept_bins, lax.axis_size('row'), chan_...  13.2 us
    reshape x2, local copies, waits for them, and re-layouts, body(): row_set.reshape(window_rows, 2, kept_bins, lax.axis_size('col'), chan_block)  12.8 us
    dot_general x1, matrix products, cross_spectra(): jnp.einsum('wcktp,ewcktq->tekpq', first_block, stacked, preferred_element...  8.24 us
    dot_general x1, matrix products, body(): jnp.einsum('wcs,sk->wkc', records, phase_table, preferred_element_type=jn...  6.06 us
  transfers between devices with their start and end apart: 3, of which 3 were waited for; matrix products, arithmetic and copies ran while one was open for 6% of the time, Pallas kernels for 0%

commit v1 on v0

--- a/solution.py
+++ b/solution.py
@@ -40,7 +40,16 @@
     whitened = (spectrum / energy).astype(jnp.bfloat16)
     whitened = lax.all_gather(whitened, "win", axis=0, tiled=True)
     row_set = lax.all_gather(whitened, "col", axis=2, tiled=True)
-    column_set = lax.all_gather(whitened, "row", axis=2, tiled=True)
+    ways = lax.axis_size("row")
+    up = [(d, (d + 1) % ways) for d in range(ways)]
+    down = [(d, (d - 1) % ways) for d in range(ways)]
+    earlier, later = ([whitened], [whitened])
+    for _ in range(ways // 2):
+        earlier.append(lax.ppermute(earlier[-1], "row", up))
+    for _ in range((ways - 1) // 2):
+        later.append(lax.ppermute(later[-1], "row", down))
+    line = jnp.concatenate([*earlier[::-1], *later[1:]], axis=2)
+    column_set = jnp.roll(line, (lax.axis_index("row") - ways // 2) * whitened.shape[2], axis=2)
     window_rows = whitened.shape[0]
     row_blocks = row_set.reshape(window_rows, 2, kept_bins, lax.axis_size("col"), chan_block)
     column_blocks = column_set.reshape(window_rows, 2, kept_bins, lax.axis_size("row"), chan_block)

time: 218 us -> 192 us (0.88)
  waiting for transfers between devices: 127 us -> 91.8 us
  starting transfers between devices: 0.08 us -> 5.46 us
  local copies, waits for them, and re-layouts: 55.6 us -> 58.7 us
    all_gather x1 -> x0, waiting for transfers between devices: 80.3 us -> none  [body(): column_set = lax.all_gather(whitened, 'row', axis=2, tiled=True)]
    ppermute x0 -> x3, waiting for transfers between devices: none -> 67.7 us  [the longest x2 48.4 us: body(): earlier.append(lax.ppermute(earlier[-1], 'row', up))]
    all_gather x1, waiting for transfers between devices: 21.6 us -> 0.01 us  [body(): row_set = lax.all_gather(whitened, 'col', axis=2, tiled=True)]
    ppermute x0 -> x3, starting transfers between devices: none -> 5.41 us  [the longest x1 3.87 us: body(): later.append(lax.ppermute(later[-1], 'row', down))]
    dynamic_slice x0 -> x1, local copies, waits for them, and re-layouts: none -> 2.68 us  [body(): jnp.roll(line, (lax.axis_index('row') - ways // 2) * whitened.shape[2], a...]
  transfers between devices with their start and end apart: 3 -> 5, of which waited for: 3 -> 4; matrix products, arithmetic and copies ran while one was open for 6% -> 13% of each run, Pallas kernels for 0% -> 0%
where the time goes in v1:
time: 192 us; the launch traced here: 191 us
  waiting for transfers between devices  91.8 us (48%)
  local copies, waits for them, and re-layouts  58.7 us (31%)
  matrix products  14.3 us (7%)
  between operations  14.2 us (7%)
  other arithmetic  6.83 us (4%)
  starting transfers between devices  5.46 us (3%)
    ppermute x2, waiting for transfers between devices, body(): earlier.append(lax.ppermute(earlier[-1], 'row', up))  48.4 us
    all_gather x1, waiting for transfers between devices, body(): whitened = lax.all_gather(whitened, 'win', axis=0, tiled=True)  24.1 us
    reshape x1, local copies, waits for them, and re-layouts, body(): summed.astype(jnp.bfloat16)  21.2 us
    ppermute x1, waiting for transfers between devices, body(): later.append(lax.ppermute(later[-1], 'row', down))  19.3 us
    reshape x2, local copies, waits for them, and re-layouts, body(): column_set.reshape(window_rows, 2, kept_bins, lax.axis_size('row'), chan_...  12.9 us
    reshape x2, local copies, waits for them, and re-layouts, body(): row_set.reshape(window_rows, 2, kept_bins, lax.axis_size('col'), chan_block)  12.8 us
    dot_general x1, matrix products, cross_spectra(): jnp.einsum('wcktp,ewcktq->tekpq', first_block, stacked, preferred_element...  8.24 us
    dot_general x1, matrix products, body(): jnp.einsum('wcs,sk->wkc', records, phase_table, preferred_element_type=jn...  6.06 us
  transfers between devices with their start and end apart: 5, of which 4 were waited for; matrix products, arithmetic and copies ran while one was open for 13% of the time, Pallas kernels for 0%

profile of v1, /device:TPU:0, one launch (start us, length us, event | category | flops | bytes accessed | tf_op | source)
XLA Modules:
  0.0 191.3 jit_solution(15525399527534338954)
XLA Ops:
  6.5 0.0 copy-start
  6.5 0.0 all-gather.3.cloned.1.call-start
  6.6 1.3 multiply_convert_fusion.1
  7.8 6.1 %multiply_reduce_fusion = (f32[16,256]{1,0:T(8,128)S(1)}, f32[64,16,256]{2,0,1:T(8,128)S(1)}) fusion(bf16[16,256,1024]{2,1,0:T(8,128)(2,1)} %param.6, bf16[1024,32]{0,1:T(8,128)(2,1)S(1)} %get-tuple-element.13, bf16[1024,32]{0,1:T(8,128)(2,1)S(1)} %get-tuple-element.12), kind=kOutput, calls=%fused_computation.14 | convolution fusion | flops 537653248 | bytes 9584640 | tf_op jit(solution)/shard_map/wcs,sk->wkc/dot_general | solution.py:38
  13.9 0.9 fusion.8
  14.8 0.0 all-gather.3.cloned.1.call-update
  14.9 0.0 all-gather.5.cloned.1.call-start
  14.9 24.1 %all-gather.3.cloned.1.call-done = bf16[32,64,256]{2,1,0:T(8,128)(2,1)} async-done(((bf16[16,64,256]{2,1,0:T(8,128)(2,1)}), bf16[32,64,256]{2,1,0:T(8,128)(2,1)}) %all-gather.3.cloned.1.call-update) | async-done | bytes 1048592 | tf_op jit(solution)/shard_map/all_gather | solution.py:41
  39.0 0.0 copy-start.2
  39.0 0.0 all-gather.5.cloned.1.call-update
  39.1 1.5 collective-permute-start
  40.6 0.0 copy-done
  40.6 0.1 constant_dynamic-slice_fusion
  40.7 0.1 copy.27
  40.8 25.2 %collective-permute-done = bf16[32,64,256]{2,1,0:T(8,128)(2,1)S(1)} collective-permute-done((bf16[32,64,256]{2,1,0:T(8,128)(2,1)}, bf16[32,64,256]{2,1,0:T(8,128)(2,1)S(1)}, u32[]{:S(2)}, u32[]{:S(2)}) %collective-permute-start) | collective-permute-done | bytes 1048608 | tf_op jit(solution)/shard_map/ppermute | solution.py:48
  66.0 0.0 collective-permute-start.1
  66.0 0.2 slice_reduce_fusion
  66.9 3.9 %collective-permute-start.2 = (bf16[32,64,256]{2,1,0:T(8,128)(2,1)}, bf16[32,64,256]{2,1,0:T(8,128)(2,1)S(1)}, u32[]{:S(2)}, u32[]{:S(2)}) collective-permute-start(bf16[32,64,256]{2,1,0:T(8,128)(2,1)} %all-gather.3.cloned.1.call-done), channel_id=1, source_target_pairs={{0,12},{4,0},{8,4},{12,8},{1,13},{5,1},{9,5},{13,9},{2,14},{6,2},{... | collective-permute-start | bytes 3145736 | tf_op jit(solution)/shard_map/ppermute | solution.py:50
  70.8 23.1 %collective-permute-done.1 = bf16[32,64,256]{2,1,0:T(8,128)(2,1)S(1)} collective-permute-done((bf16[32,64,256]{2,1,0:T(8,128)(2,1)S(1)}, bf16[32,64,256]{2,1,0:T(8,128)(2,1)S(1)}, u32[]{:S(2)}, u32[]{:S(2)}) %collective-permute-start.1) | collective-permute-done | bytes 1048608 | tf_op jit(solution)/shard_map/ppermute | solution.py:48
  93.9 0.1 constant_dynamic-update-slice_fusion.7
  94.1 0.1 constant_dynamic-update-slice_fusion.6
  94.2 0.0 copy-done.2
  94.2 0.1 constant_dynamic-update-slice_fusion.5
  94.4 19.3 %collective-permute-done.2 = bf16[32,64,256]{2,1,0:T(8,128)(2,1)S(1)} collective-permute-done((bf16[32,64,256]{2,1,0:T(8,128)(2,1)}, bf16[32,64,256]{2,1,0:T(8,128)(2,1)S(1)}, u32[]{:S(2)}, u32[]{:S(2)}) %collective-permute-start.2) | collective-permute-done | bytes 1048608 | tf_op jit(solution)/shard_map/ppermute | solution.py:50
  113.7 0.1 constant_dynamic-update-slice_fusion.4
  113.8 0.1 constant_dynamic-update-slice_fusion.3
  113.9 0.1 constant_dynamic-update-slice_fusion.2
  114.1 0.1 constant_dynamic-update-slice_fusion.1
  114.2 0.1 constant_dynamic-update-slice_fusion
  114.4 2.7 %constant_dynamic-slice_fusion.1 = bf16[32,64,1024]{2,1,0:T(8,128)(2,1)} fusion(bf16[32,64,2048]{2,1,0:T(8,128)(2,1)S(1)} %constant_dynamic-update-slice_fusion, s32[]{:T(128)S(6)} %select_n.31), kind=kLoop, calls=%fused_computation.54 | loop fusion | bytes 8388612 | tf_op jit(solution)/shard_map/jit(_roll_dynamic)/dynamic_slice | solution.py:52
  117.1 7.9 %reshape.42 = bf16[32,2,32,4,256]{4,3,2,1,0:T(4,128)(2,1)} reshape(bf16[32,64,1024]{2,1,0:T(8,128)(2,1)} %constant_dynamic-slice_fusion.1) | data formatting | bytes 8388608 | tf_op jit(solution)/shard_map/reshape | solution.py:55
  125.0 5.0 %copy.28 = bf16[32,2,32,4,256]{4,2,1,0,3:T(8,128)(2,1)} copy(bf16[32,2,32,4,256]{4,3,2,1,0:T(4,128)(2,1)} %reshape.42) | data formatting | bytes 8388608 | tf_op jit(solution)/shard_map/reshape | solution.py:55
  130.0 2.9 %gather_fusion = bf16[2,32,2,32,256]{4,3,2,1,0:T(8,128)(2,1)S(1)} fusion(bf16[32,2,32,4,256]{4,2,1,0,3:T(8,128)(2,1)} %copy.28, s32[1024]{0:T(1024)S(1)} %pad_clamp_fusion.1), kind=kCustom, calls=%fused_computation.clone | custom fusion | bytes 4194312 | tf_op jit(solution)/shard_map/jit(_take)/gather | solution.py:63
  132.9 2.7 %fusion.6 = (bf16[1,32,2,32,2,256]{5,1,2,0,3,4:T(8,128)(2,1)}, bf16[32,2,32,2,256]{4,0,1,2,3:T(8,128)(2,1)S(1)}) fusion(bf16[2,32,2,32,256]{4,3,2,1,0:T(8,128)(2,1)S(1)} %gather_fusion, pred[2]{0:T(512)(128)(4,1)S(1)} %get-tuple-element.19), kind=kLoop, calls=%fused_computation.15 | loop fusion | flops 1048576 | bytes 6291458 | tf_op jit(solution)/shard_map/stack | solution.py:21
  135.5 0.1 slice_negate_fusion
  135.6 1.5 maximum_bitcast_fusion
  137.2 0.0 all-gather.5.cloned.1.call-done
  137.2 7.8 %reshape.43 = bf16[32,2,32,4,256]{4,3,2,1,0:T(4,128)(2,1)} reshape(bf16[32,64,1024]{2,1,0:T(8,128)(2,1)} %all-gather.5.cloned.1.call-done) | data formatting | bytes 8388608 | tf_op jit(solution)/shard_map/reshape | solution.py:54
  145.0 4.9 %copy.31 = bf16[32,2,32,4,256]{4,2,1,0,3:T(8,128)(2,1)} copy(bf16[32,2,32,4,256]{4,3,2,1,0:T(4,128)(2,1)} %reshape.43) | data formatting | bytes 8388608 | tf_op jit(solution)/shard_map/reshape | solution.py:54
  149.9 2.9 %gather_fusion.1 = bf16[2,32,2,32,256]{4,3,2,1,0:T(8,128)(2,1)S(1)} fusion(bf16[32,2,32,4,256]{4,2,1,0,3:T(8,128)(2,1)} %copy.31, s32[1024]{0:T(1024)S(1)} %pad_clamp_fusion), kind=kCustom, calls=%fused_computation.1.clone | custom fusion | bytes 4194312 | tf_op jit(solution)/shard_map/jit(_take)/gather | solution.py:62
  152.8 0.0 copy-start.3
  152.8 0.0 copy-start.4
  152.8 0.3 select_bitcast_fusion
  153.1 1.3 copy-done.3
  154.4 0.6 copy-done.4
  155.0 8.2 %fusion.1 = bf16[1,1,2,2,32,256,256]{5,6,3,4,2,1,0:T(8,128)(2,1)} fusion(f32[2]{0:T(128)S(1)} %compare_convert_fusion, bf16[1,32,2,32,2,256]{5,1,2,0,3,4:T(8,128)(2,1)S(1)} %copy-done.4, bf16[1,32,2,32,2,256]{5,1,2,0,3,4:T(8,128)(2,1)S(1)} %copy-done.3, bf16[32,2,32,2,256,1]{4,2,1,0,3,5:T(8,128)(2,1)S(1)} %select_bitcast_fusion), kind=kOutput, calls=%fused_computation.4 | convolution fusion | flops 1092616192 | bytes 23068680 | tf_op jit(solution)/shard_map/wcktp,ewcktq->tekpq/dot_general | solution.py:28
  163.3 21.2 %copy.33 = bf16[1,1,2,2,32,256,256]{6,5,4,3,2,1,0:T(8,128)(2,1)} copy(bf16[1,1,2,2,32,256,256]{5,6,3,4,2,1,0:T(8,128)(2,1)} %fusion.1) | data formatting | bytes 33554432 | tf_op jit(solution)/shard_map/reshape | solution.py:66
  184.5 0.0 copy-done.1
  (9 shorter events, 0.1 us)
Async XLA Ops:
  6.5 34.1 %copy-start = (s32[1,1,4,2]{2,3,1,0:T(2,128)S(1)}, s32[1,1,4,2]{2,3,1,0:T(2,128)}, u32[]{:S(2)}) copy-start(s32[1,1,4,2]{2,3,1,0:T(2,128)} %param.7) | copy-start | bytes 100
  6.5 32.5 %all-gather.3.cloned.1.call-start = ((), (), s32[]{:S(2)}) async-start(), calls=%async_computation | async-start | bytes 1572864 | tf_op jit(solution)/shard_map/all_gather | solution.py:41
  14.9 122.3 %all-gather.5.cloned.1.call-start = ((), (), s32[]{:S(2)}) async-start(), calls=%async_computation.1 | async-start | bytes 5242880 | tf_op jit(solution)/shard_map/all_gather | solution.py:42
  39.0 55.2 %copy-start.2 = (bf16[32,64,256]{2,1,0:T(8,128)(2,1)S(1)}, bf16[32,64,256]{2,1,0:T(8,128)(2,1)}, u32[]{:S(2)}) copy-start(bf16[32,64,256]{2,1,0:T(8,128)(2,1)} %all-gather.3.cloned.1.call-done) | copy-start | bytes 3145732
  39.1 27.0 %collective-permute-start = (bf16[32,64,256]{2,1,0:T(8,128)(2,1)}, bf16[32,64,256]{2,1,0:T(8,128)(2,1)S(1)}, u32[]{:S(2)}, u32[]{:S(2)}) collective-permute-start(bf16[32,64,256]{2,1,0:T(8,128)(2,1)} %all-gather.3.cloned.1.call-done), channel_id=1, source_target_pairs={{0,4},{4,8},{8,12},{12,0},{1,5},{5,9},{9,13},{13,1},{2,6},{6,10},{... | collective-permute-start | bytes 3145736 | tf_op jit(solution)/shard_map/ppermute | solution.py:48
  66.0 27.9 %collective-permute-start.1 = (bf16[32,64,256]{2,1,0:T(8,128)(2,1)S(1)}, bf16[32,64,256]{2,1,0:T(8,128)(2,1)S(1)}, u32[]{:S(2)}, u32[]{:S(2)}) collective-permute-start(bf16[32,64,256]{2,1,0:T(8,128)(2,1)S(1)} %collective-permute-done), channel_id=1, source_target_pairs={{0,4},{4,8},{8,12},{12,0},{1,5},{5,9},{9,13},{13,1},{2,6},{6,10},{... | collective-permute-start | bytes 3145736 | tf_op jit(solution)/shard_map/ppermute | solution.py:48
  66.9 46.8 %collective-permute-start.2 = (bf16[32,64,256]{2,1,0:T(8,128)(2,1)}, bf16[32,64,256]{2,1,0:T(8,128)(2,1)S(1)}, u32[]{:S(2)}, u32[]{:S(2)}) collective-permute-start(bf16[32,64,256]{2,1,0:T(8,128)(2,1)} %all-gather.3.cloned.1.call-done), channel_id=1, source_target_pairs={{0,12},{4,0},{8,4},{12,8},{1,13},{5,1},{9,5},{13,9},{2,14},{6,2},{... | collective-permute-start | bytes 3145736 | tf_op jit(solution)/shard_map/ppermute | solution.py:50
  152.8 1.6 copy-start.3
  152.8 2.2 %copy-start.4 = (bf16[1,32,2,32,2,256]{5,1,2,0,3,4:T(8,128)(2,1)S(1)}, bf16[1,32,2,32,2,256]{5,1,2,0,3,4:T(8,128)(2,1)}, u32[]{:S(2)}) copy-start(bf16[1,32,2,32,2,256]{5,1,2,0,3,4:T(8,128)(2,1)} %maximum_bitcast_fusion) | copy-start | bytes 6291460
  163.3 21.2 %copy-start.1 = (s32[1,1,4,2]{2,3,1,0:T(2,128)S(1)}, s32[1,1,4,2]{2,3,1,0:T(2,128)}, u32[]{:S(2)}) copy-start(s32[1,1,4,2]{2,3,1,0:T(2,128)} %param.7) | copy-start | bytes 100
Sparse Core Ops, SparseCore 0:
  15.0 23.9 all-gather.2
  40.6 35.0 all-gather.4
